TPU v7x, 32 devices: a whole 2x2x4 slice. The times are simulated.
32 devices in a mesh: rep: 2 (over y), chol: 8 (over z, x), pop: 2 (over core).
Axes of the slice: x: 2, y: 2, z: 4, core: 2. Of those that a mesh axis runs over, the one named last changes fastest.
Arguments:
- green_half: bfloat16 [256, 16, 1024], P(('rep', 'chol'), 'pop'), parts along dimension 0, may hold values from -5 to 5
- step_delta: bfloat16 [256, 16, 1024], P(('rep', 'chol'), 'pop'), parts along dimension 0, may hold values from -4 to 4
- chol_vectors: bfloat16 [96, 128, 1024], P(('rep', 'chol')), parts along dimension 0, as said below
- copy_counts: int32 [32], P(('rep', 'pop')), parts along dimension 0, may hold values from 0 to 2, as said below
- parents: int32 [32], P('rep'), parts along dimension 0, may hold values from 0 to 15, as said below
Outputs:
- parent_force: bfloat16 [256, 16, 1024], P(('rep', 'chol'), 'pop'), parts along dimension 0
- child_energy: float32 [32], P(('rep', 'pop')), parts along dimension 0
There are 2 independent parts, one for each index of `rep`. A program takes and returns all parts, laid end to end along the dimension named above; each array names one. Nothing has to cross between parts.
Inputs may be any that keep to these rules, and one draw needn't show every extreme that they name: copy_counts[p] is the number of children c with parents[c] = p; the counts sum to 16; some walker has 0 copies and some has 2. parents never falls from one child to the next; the first child's parent is walker 0 and the last child's is walker 16 - 1; each child's parent is the child itself or a walker next to it. `chol_vectors`: entries are of order 1 / sqrt(1024) times a factor per vector.
All inputs are finite; a program needn't handle non-finite values.
Results may differ from a plain program's by a relative error of at most 0.0057.
Values may be sent and summed in bfloat16 or wider, within the bound.
A program may use at most 64 MiB of HBM per device.

v0:
```python
import jax
import jax.numpy as jnp
from jax import lax
from jax.sharding import PartitionSpec as P


def child_forces(child_rows, chol_vectors):
    total_chol = lax.axis_size("chol") * chol_vectors.shape[0]
    orbitals = chol_vectors.shape[1]
    factor = -1.0 / total_chol**0.5
    cross = jnp.einsum(
        "iwm,gkm->wgik",
        lax.all_gather(child_rows, "chol", axis=0, tiled=True),
        chol_vectors,
        preferred_element_type=jnp.float32,
    )
    cross_low = cross.astype(jnp.bfloat16)
    trace_part = jnp.sum(cross_low.astype(jnp.float32) * jnp.swapaxes(cross, 2, 3), axis=(1, 2, 3))
    energies = lax.psum(trace_part, "chol") * (-0.125 / (total_chol * orbitals))
    forces = lax.psum_scatter(
        factor
        * jnp.einsum("wgik,gil->kwl", cross_low, chol_vectors, preferred_element_type=jnp.float32),
        "chol",
        scatter_dimension=0,
        tiled=True,
    )
    return (forces, energies)


def shards(green_half, step_delta, chol_vectors, copy_counts, parents):
    per_group = green_half.shape[1]
    my_group = lax.axis_index("pop")
    all_parents = lax.all_gather(green_half, "pop", axis=1, tiled=True)
    my_parents = lax.dynamic_slice_in_dim(parents, my_group * per_group, per_group, 0)
    picked = jnp.take(all_parents, my_parents, axis=1)
    child_rows = (picked.astype(jnp.float32) + step_delta.astype(jnp.float32)).astype(jnp.bfloat16)
    forces, child_energy = child_forces(child_rows, chol_vectors)
    parent_slots = jnp.arange(all_parents.shape[1], dtype=jnp.int32)
    one_hot = (my_parents[:, None] == parent_slots[None, :]).astype(jnp.float32)
    spread_sum = jnp.einsum("kcl,cp->kpl", forces, one_hot, precision=lax.Precision.HIGHEST)
    summed = lax.psum_scatter(
        spread_sum.astype(jnp.bfloat16), "pop", scatter_dimension=1, tiled=True
    ).astype(jnp.float32)
    divisor = jnp.maximum(copy_counts, 1).astype(jnp.float32)
    parent_force = (summed / divisor[None, :, None]).astype(jnp.bfloat16)
    return (parent_force, child_energy)


def solution(mesh):
    placed = (
        P(("rep", "chol"), "pop", None),
        P(("rep", "chol"), "pop", None),
        P(("rep", "chol"), None, None),
        P(("rep", "pop")),
        P("rep"),
    )
    return jax.shard_map(
        shards,
        mesh=mesh,
        in_specs=placed,
        out_specs=(P(("rep", "chol"), "pop", None), P(("rep", "pop"))),
        check_vma=False,
    )
```

profile of v0, /device:TPU:0, one launch (start us, length us, event | category | flops | bytes accessed | tf_op | source)
XLA Modules:
  0.0 200.1 jit_solution(10140148454134975088)
XLA Ops:
  7.2 0.0 copy-start
  7.2 0.0 all-gather.2.cloned.1.call-start
  7.2 0.8 compare_and_fusion
  8.1 1.1 copy.12
  9.2 2.3 %all_gather.6 = bf16[16,16,1024]{2,0,1:T(8,128)(2,1)S(1)} all-gather(bf16[16,8,1024]{2,0,1:T(8,128)(2,1)S(1)} %copy.12), channel_id=1, replica_groups=mesh['rep'=2,'chol'=8,'pop'=2] {'pop'}, dimensions={1}, use_global_device_ids=true | all-gather | bytes 786432 | tf_op jit(solution)/shard_map/all_gather | solution.py:33
  11.5 0.6 gather_fusion
  12.0 1.9 fusion.8
  13.9 0.0 all-gather.2.cloned.1.call-update
  13.9 0.0 reduce-scatter.5.cloned.1.call-start
  14.0 52.0 %all-gather.2.cloned.1.call-done = bf16[128,8,1024]{2,0,1:T(8,128)(2,1)} async-done(((bf16[16,8,1024]{2,0,1:T(8,128)(2,1)}), bf16[128,8,1024]{2,0,1:T(8,128)(2,1)}) %all-gather.2.cloned.1.call-update) | async-done | bytes 2097168 | tf_op jit(solution)/shard_map/all_gather | solution.py:13
  65.9 0.0 copy-done
  65.9 5.1 %fusion.2 = f32[128,8,6,128]{3,0,2,1:T(8,128)} fusion(bf16[128,8,1024]{2,0,1:T(8,128)(2,1)} %all-gather.2.cloned.1.call-done, bf16[6,128,1024]{2,1,0:T(8,128)(2,1)S(1)} %copy-done), kind=kOutput, calls=%fused_computation.5 | convolution fusion | flops 1610612736 | bytes 6815744 | tf_op jit(solution)/shard_map/iwm,gkm->wgik/dot_general | solution.py:11
  71.0 2.3 %copy.14 = bf16[128,8,6,128]{0,3,2,1:T(8,128)(2,1)S(1)} copy(f32[128,8,6,128]{3,0,2,1:T(8,128)} %fusion.2) | data formatting | bytes 4718592 | tf_op jit(solution)/shard_map/iwm,gkm->wgik/dot_general | solution.py:11
  73.3 5.8 %fusion = f32[128,8,1024]{2,1,0:T(8,128)} fusion(bf16[6,128,1024]{2,1,0:T(8,128)(2,1)S(1)} %copy-done, bf16[8,6,128,128]{2,3,1,0:T(8,128)(2,1)S(1)} %bitcast.51), kind=kOutput, calls=%fused_computation.2 | convolution fusion | flops 1611661312 | bytes 7340032 | tf_op jit(solution)/shard_map/wgik,gil->kwl/dot_general | solution.py:22
  79.2 0.0 reduce-scatter.5.cloned.1.call-update
  79.2 0.0 reduce-scatter.7.cloned.1.call-start
  79.2 86.7 %reduce-scatter.5.cloned.1.call-done = f32[16,8,1024]{2,1,0:T(8,128)} async-done(((f32[128,8,1024]{2,1,0:T(8,128)}), f32[16,8,1024]{2,1,0:T(8,128)}) %reduce-scatter.5.cloned.1.call-update) | async-done | bytes 524304 | tf_op jit(solution)/shard_map/reduce_scatter | solution.py:20
  165.9 1.7 fusion.12
  167.7 0.8 copy.20
  168.5 0.0 reduce-scatter.7.cloned.1.call-update
  168.5 0.0 copy-start.1
  168.5 2.4 %fusion.1 = f32[8]{0:T(128)S(1)} fusion(f32[128,8,6,128]{3,0,2,1:T(8,128)} %fusion.2, bf16[128,8,6,128]{0,3,2,1:T(8,128)(2,1)S(1)} %copy.14), kind=kLoop, calls=%fused_computation.4 | loop fusion | flops 2359288 | bytes 4718624 | tf_op jit(solution)/shard_map/reduce_sum | solution.py:18
  170.9 0.0 copy-done.1
  170.9 20.2 %psum.7 = f32[8]{0:T(128)S(1)} all-reduce(f32[8]{0:T(128)S(1)} %fusion.1), channel_id=1, replica_groups=mesh['rep'=2,'chol'=8,'pop'=2] {'chol'}, use_global_device_ids=true, to_apply=%region_3.4 | all-reduce | flops 8 | bytes 64 | tf_op jit(solution)/shard_map/psum | solution.py:19
  191.1 0.5 broadcast_multiply_fusion
  191.6 0.0 reduce-scatter.7.cloned.1.call-done
  191.6 1.1 copy.28
  192.7 0.9 divide_convert_fusion
  (3 shorter events, 0.0 us)
Async XLA Ops:
  7.2 58.8 %copy-start = (bf16[6,128,1024]{2,1,0:T(8,128)(2,1)S(1)}, bf16[6,128,1024]{2,1,0:T(8,128)(2,1)}, u32[]{:S(2)}) copy-start(bf16[6,128,1024]{2,1,0:T(8,128)(2,1)} %param.7) | copy-start | bytes 4718596
  7.2 58.8 %all-gather.2.cloned.1.call-start = ((), (), s32[]{:S(2)}) async-start(), calls=%async_computation.2 | async-start | bytes 2359296 | tf_op jit(solution)/shard_map/all_gather | solution.py:13
  13.9 152.0 %reduce-scatter.5.cloned.1.call-start = ((), (), s32[]{:S(2)}) async-start(), calls=%async_computation.3 | async-start | bytes 4718592 | tf_op jit(solution)/shard_map/reduce_scatter | solution.py:20
  79.2 112.4 %reduce-scatter.7.cloned.1.call-start = ((), (), s32[]{:S(2)}) async-start(), calls=%async_computation.4 | async-start | bytes 786432
  168.5 2.4 %copy-start.1 = (s32[8]{0:T(128)S(1)}, s32[8]{0:T(128)}, u32[]{:S(2)}) copy-start(s32[8]{0:T(128)} %param.8) | copy-start | bytes 100
Sparse Core Ops, SparseCore 0:
  14.0 51.8 all-gather.1
  79.3 86.5 reduce-scatter.4
  168.6 7.7 reduce-scatter.6
where the time goes:
time: 200 us
  waiting for transfers between devices  139 us (70%)
  blocking collectives  22.4 us (11%)
  between operations  13.8 us (7%)
  matrix products  12.6 us (6%)
  other arithmetic  6.49 us (3%)
  local copies, waits for them, and re-layouts  5.9 us (3%)
    reduce_scatter x1, waiting for transfers between devices, child_forces(): lax.psum_scatter(factor * jnp.einsum('wgik,gil->kwl', cross_low, chol_vec...  86.7 us
    all_gather x1, waiting for transfers between devices, child_forces(): lax.all_gather(child_rows, 'chol', axis=0, tiled=True)  52 us
    psum x1, blocking collectives, child_forces(): energies = lax.psum(trace_part, 'chol') * (-0.125 / (total_chol * orbitals))  20.2 us
    dot_general x1, matrix products, child_forces(): jnp.einsum('wgik,gil->kwl', cross_low, chol_vectors, preferred_element_ty...  5.82 us
    dot_general x1, matrix products, child_forces(): jnp.einsum('iwm,gkm->wgik', lax.all_gather(child_rows, 'chol', axis=0, ti...  5.09 us
  transfers between devices with their start and end apart: 3, of which 2 were waited for; matrix products, arithmetic and copies ran while one was open for 1% of the time, Pallas kernels for 0%

commit v1 on v0

--- a/solution.py
+++ b/solution.py
@@ -1,7 +1,14 @@
+import functools
+
 import jax
 import jax.numpy as jnp
 from jax import lax
+from jax.experimental import pallas as pl
+from jax.experimental.pallas import tpu as pltpu
 from jax.sharding import PartitionSpec as P
+
+MESH = pl.DeviceIdType.MESH
+CHUNK = 2
 
 
 def child_forces(child_rows, chol_vectors):
@@ -46,6 +53,341 @@
     return (parent_force, child_energy)
 
 
+def ring_device(pos, n):
+    half = n // 2
+    pos = lax.rem(pos + 2 * n, n)
+    side = lax.div(pos, half)
+    rest = lax.rem(pos, half)
+    return 2 * ((1 - side) * rest + side * (half - 1 - rest)) + side
+
+
+def step_kernel(
+    n, parents, counts, green, delta, chol, out, energy_out,
+    gpad, gall, cross, force, fsend, arrived, final, edge, traces,
+    ag_send, ag_recv, rs_send, rs_recv, tr_send, tr_recv, edge_send, edge_recv,
+):
+    walkers, rows, basis = green.shape
+    vectors, orbitals, _ = chol.shape
+    chunks = walkers // CHUNK
+    me = lax.axis_index("chol")
+    pop = lax.axis_index("pop")
+    side = lax.rem(me, 2)
+    level = lax.div(me, 2)
+    pos = side * (n - 1 - level) + (1 - side) * level
+    hops = (n // 2, n - 1 - n // 2)
+    scale = -1.0 / (n * vectors) ** 0.5
+
+    def first_walker(ch):
+        late = jnp.minimum(lax.div(ch, 2), 1)
+        k = late * ch + (1 - late) * (1 - ch)
+        return CHUNK * (pop * k + (1 - pop) * (chunks - 1 - k))
+
+    def sign(ch, chain):
+        up = 1 - 2 * lax.rem(ch, 2)
+        return up if chain == 0 else -up
+
+    def orbital_rows(device):
+        return pl.ds(pl.multiple_of(device * rows, rows), rows)
+
+    def gather(ch, chain, step):
+        way = sign(ch, chain)
+        where = (pl.ds(first_walker(ch), CHUNK), orbital_rows(ring_device(pos - way * step, n)))
+        return pltpu.make_async_remote_copy(
+            src_ref=gall.at[where],
+            dst_ref=gall.at[where],
+            send_sem=ag_send.at[chain, step, ch],
+            recv_sem=ag_recv.at[chain, step, ch],
+            device_id={"chol": ring_device(pos + way, n)},
+            device_id_type=MESH,
+        )
+
+    def gather_arrival(ch, chain, step):
+        way = sign(ch, chain)
+        where = (pl.ds(first_walker(ch), CHUNK), orbital_rows(ring_device(pos - way * (step + 1), n)))
+        return pltpu.make_async_remote_copy(
+            src_ref=gall.at[where],
+            dst_ref=gall.at[where],
+            send_sem=ag_send.at[chain, step, ch],
+            recv_sem=ag_recv.at[chain, step, ch],
+            device_id={"chol": ring_device(pos + way, n)},
+            device_id_type=MESH,
+        )
+
+    def scatter(ch, chain, step):
+        way = sign(ch, chain)
+        target = orbital_rows(ring_device(pos + way * (hops[chain] - step), n))
+        return pltpu.make_async_remote_copy(
+            src_ref=fsend.at[pl.ds(first_walker(ch), CHUNK), target],
+            dst_ref=arrived.at[chain, step, ch],
+            send_sem=rs_send.at[chain, step, ch],
+            recv_sem=rs_recv.at[chain, step, ch],
+            device_id={"chol": ring_device(pos + way, n)},
+            device_id_type=MESH,
+        )
+
+    def start_scatter(ch, chain, step):
+        way = sign(ch, chain)
+        target = orbital_rows(ring_device(pos + way * (hops[chain] - step), n))
+        w0 = first_walker(ch)
+        for j in range(CHUNK):
+            part = force[w0 + j, target, :]
+            if step > 0:
+                part = part + arrived[chain, step - 1, ch, j].astype(jnp.float32)
+            fsend[w0 + j, target, :] = part.astype(jnp.bfloat16)
+        scatter(ch, chain, step).start()
+
+    def trace_copy(offset, owner, peer):
+        return pltpu.make_async_remote_copy(
+            src_ref=traces.at[owner],
+            dst_ref=traces.at[owner],
+            send_sem=tr_send.at[offset],
+            recv_sem=tr_recv.at[offset],
+            device_id={"chol": peer},
+            device_id_type=MESH,
+        )
+
+    barrier = pltpu.get_barrier_semaphore()
+    for offset in range(1, n):
+        pl.semaphore_signal(
+            barrier, inc=1, device_id={"chol": lax.rem(me + offset, n)}, device_id_type=MESH
+        )
+    pl.semaphore_signal(barrier, inc=1, device_id={"pop": 1 - pop}, device_id_type=MESH)
+    gpad[pop * (walkers + 1)] = jnp.zeros((rows, basis), jnp.bfloat16)
+    gpad[pl.ds(1, walkers)] = green[...]
+    pl.semaphore_wait(barrier, n)
+
+    edge_green = pltpu.make_async_remote_copy(
+        src_ref=green.at[(1 - pop) * (walkers - 1)],
+        dst_ref=gpad.at[pop * (walkers + 1)],
+        send_sem=edge_send.at[0],
+        recv_sem=edge_recv.at[0],
+        device_id={"pop": 1 - pop},
+        device_id_type=MESH,
+    )
+    edge_green_arrival = pltpu.make_async_remote_copy(
+        src_ref=green.at[(1 - pop) * (walkers - 1)],
+        dst_ref=gpad.at[(1 - pop) * (walkers + 1)],
+        send_sem=edge_send.at[0],
+        recv_sem=edge_recv.at[0],
+        device_id={"pop": 1 - pop},
+        device_id_type=MESH,
+    )
+    edge_green.start()
+
+    for ch in range(chunks):
+        if ch == 1:
+            edge_green_arrival.wait_recv()
+        w0 = first_walker(jnp.int32(ch))
+        for j in range(CHUNK):
+            child = pop * walkers + w0 + j
+            parent = parents[child]
+            row = delta[w0 + j].astype(jnp.float32)
+            for k in range(3):
+                chosen = jnp.where(parent == child - 1 + k, 1.0, 0.0)
+                row = row + chosen * gpad[w0 + j + k].astype(jnp.float32)
+            gall[w0 + j, orbital_rows(me), :] = row.astype(jnp.bfloat16)
+        for chain in range(2):
+            gather(jnp.int32(ch), chain, 0).start()
+
+    for step in range(1, hops[0]):
+
+        def forward(ch, carry, step=step):
+            for chain in range(2):
+                if step < hops[chain]:
+                    gather_arrival(ch, chain, step - 1).wait_recv()
+                    gather(ch, chain, step).start()
+            return carry
+
+        lax.fori_loop(0, chunks, forward, 0)
+
+    row_ids = lax.broadcasted_iota(jnp.int32, (orbitals, 2 * orbitals), 0)
+    col_ids = lax.broadcasted_iota(jnp.int32, (orbitals, 2 * orbitals), 1)
+    diagonal = (row_ids == col_ids) | (row_ids + orbitals == col_ids)
+    walker_ids = lax.broadcasted_iota(jnp.int32, (walkers, orbitals), 0)
+
+    def compute(ch, total):
+        for chain in range(2):
+            gather_arrival(ch, chain, hops[chain] - 1).wait_recv()
+        w0 = first_walker(ch)
+        children = gall[pl.ds(w0, CHUNK)].reshape(CHUNK * orbitals, basis)
+        turned = lax.dot_general(
+            chol[...].reshape(vectors * orbitals, basis),
+            children,
+            (((1,), (1,)), ((), ())),
+            preferred_element_type=jnp.float32,
+        )
+        low = turned.astype(jnp.bfloat16)
+        rest = (turned - low.astype(jnp.float32)).astype(jnp.bfloat16)
+        for j in range(CHUNK):
+            mine = slice(j * orbitals, (j + 1) * orbitals)
+            for g in range(vectors):
+                cross[mine, g * orbitals : (g + 1) * orbitals] = low[
+                    g * orbitals : (g + 1) * orbitals, mine
+                ]
+            products = jnp.dot(
+                cross[mine, :],
+                jnp.concatenate([low[:, mine], rest[:, mine]], axis=1),
+                preferred_element_type=jnp.float32,
+            )
+            line = jnp.sum(jnp.where(diagonal, products, 0.0), axis=0, keepdims=True)
+            line = line[:, :orbitals] + line[:, orbitals:]
+            total = total + jnp.where(walker_ids == w0 + j, line, 0.0)
+        force[pl.ds(w0, CHUNK)] = jnp.dot(
+            cross[...],
+            chol[...].reshape(vectors * orbitals, basis),
+            preferred_element_type=jnp.float32,
+        ).reshape(CHUNK, orbitals, basis)
+        for chain in range(2):
+            start_scatter(ch, chain, 0)
+        return total
+
+    traces[me] = lax.fori_loop(0, chunks, compute, jnp.zeros((walkers, orbitals), jnp.float32))
+    for offset in range(1, n):
+        trace_copy(offset - 1, me, lax.rem(me + offset, n)).start()
+
+    for step in range(1, hops[0]):
+
+        def add_and_forward(ch, carry, step=step):
+            for chain in range(2):
+                if step < hops[chain]:
+                    scatter(ch, chain, step - 1).wait_recv()
+                    start_scatter(ch, chain, step)
+            return carry
+
+        lax.fori_loop(0, chunks, add_and_forward, 0)
+
+    edge_force = pltpu.make_async_remote_copy(
+        src_ref=edge.at[0],
+        dst_ref=edge.at[1],
+        send_sem=edge_send.at[1],
+        recv_sem=edge_recv.at[1],
+        device_id={"pop": 1 - pop},
+        device_id_type=MESH,
+    )
+    final[pop * (walkers + 1)] = jnp.zeros((rows, basis), jnp.float32)
+    for ch in range(chunks):
+        at = jnp.int32(ch)
+        w0 = first_walker(at)
+        for chain in range(2):
+            scatter(at, chain, hops[chain] - 1).wait_recv()
+        for j in range(CHUNK):
+            final[w0 + j + 1] = scale * (
+                force[w0 + j, orbital_rows(me), :]
+                + arrived[0, hops[0] - 1, ch, j].astype(jnp.float32)
+                + arrived[1, hops[1] - 1, ch, j].astype(jnp.float32)
+            )
+        if ch == 1:
+            edge[0] = final[1 + (1 - pop) * (walkers - 1)].astype(jnp.bfloat16)
+            edge_force.start()
+
+    edge_force.wait_recv()
+    final[(1 - pop) * (walkers + 1)] = edge[1].astype(jnp.float32)
+    for w in range(walkers):
+        parent = pop * walkers + w
+        row = jnp.zeros((rows, basis), jnp.float32)
+        for k in range(3):
+            child = parent - 1 + k
+            inside = (child >= 0) & (child < 2 * walkers)
+            taken = parents[jnp.minimum(jnp.maximum(child, 0), 2 * walkers - 1)] == parent
+            row = row + jnp.where(inside & taken, 1.0, 0.0) * final[w + k]
+        copies = jnp.maximum(counts[w], 1).astype(jnp.float32)
+        out[w] = (row / jnp.full((rows, basis), copies)).astype(jnp.bfloat16)
+
+    for offset in range(1, n):
+        trace_copy(offset - 1, lax.rem(me + n - offset, n), me).wait_recv()
+    energy = traces[0]
+    for i in range(1, n):
+        energy = energy + traces[i]
+    energy_out[...] = energy
+
+    edge_green.wait_send()
+    edge_force.wait_send()
+    for offset in range(1, n):
+        trace_copy(offset - 1, me, lax.rem(me + offset, n)).wait_send()
+
+    def drain(ch, carry):
+        for chain in range(2):
+            for step in range(hops[chain]):
+                gather(ch, chain, step).wait_send()
+                scatter(ch, chain, step).wait_send()
+        return carry
+
+    lax.fori_loop(0, chunks, drain, 0)
+
+
+def ring_shards(green_half, step_delta, chol_vectors, copy_counts, parents):
+    n = lax.axis_size("chol")
+    rows, walkers, basis = green_half.shape
+    vectors, orbitals, _ = chol_vectors.shape
+    chunks = walkers // CHUNK
+    hops = n // 2
+    smem = pl.BlockSpec(memory_space=pltpu.SMEM)
+    vmem = pl.BlockSpec(memory_space=pltpu.VMEM)
+    dma = pltpu.SemaphoreType.DMA
+    wide = vectors * orbitals
+    out, traces = pl.pallas_call(
+        functools.partial(step_kernel, n),
+        out_shape=(
+            jax.ShapeDtypeStruct((walkers, rows, basis), jnp.bfloat16),
+            jax.ShapeDtypeStruct((walkers, orbitals), jnp.float32),
+        ),
+        in_specs=[smem, smem, vmem, vmem, vmem],
+        out_specs=(vmem, vmem),
+        scratch_shapes=[
+            pltpu.VMEM((walkers + 2, rows, basis), jnp.bfloat16),
+            pltpu.VMEM((walkers, orbitals, basis), jnp.bfloat16),
+            pltpu.VMEM((CHUNK * orbitals, wide), jnp.bfloat16),
+            pltpu.VMEM((walkers, orbitals, basis), jnp.float32),
+            pltpu.VMEM((walkers, orbitals, basis), jnp.bfloat16),
+            pltpu.VMEM((2, hops, chunks, CHUNK, rows, basis), jnp.bfloat16),
+            pltpu.VMEM((walkers + 2, rows, basis), jnp.float32),
+            pltpu.VMEM((2, rows, basis), jnp.bfloat16),
+            pltpu.VMEM((n, walkers, orbitals), jnp.float32),
+            dma((2, hops, chunks)),
+            dma((2, hops, chunks)),
+            dma((2, hops, chunks)),
+            dma((2, hops, chunks)),
+            dma((n - 1,)),
+            dma((n - 1,)),
+            dma((2,)),
+            dma((2,)),
+        ],
+        compiler_params=pltpu.CompilerParams(
+            collective_id=0, has_side_effects=True, vmem_limit_bytes=40 * 1024 * 1024
+        ),
+        cost_estimate=pl.CostEstimate(
+            flops=4 * walkers * orbitals * wide * basis,
+            bytes_accessed=4 * walkers * orbitals * basis,
+            transcendentals=0,
+        ),
+    )(
+        parents,
+        copy_counts,
+        jnp.swapaxes(green_half, 0, 1),
+        jnp.swapaxes(step_delta, 0, 1),
+        chol_vectors,
+    )
+    energy = jnp.sum(traces, axis=1) * (-0.125 / (n * vectors * orbitals))
+    return jnp.swapaxes(out, 0, 1), energy
+
+
+def any_shards(green_half, step_delta, chol_vectors, copy_counts, parents):
+    rows, walkers, basis = green_half.shape
+    orbitals = chol_vectors.shape[1]
+    n = lax.axis_size("chol")
+    fits = (
+        rows % 16 == 0
+        and orbitals % 128 == 0
+        and basis % 128 == 0
+        and walkers == 4 * CHUNK
+        and n % 2 == 0
+        and n >= 4
+        and lax.axis_size("pop") == 2
+    )
+    run = ring_shards if fits else shards
+    return run(green_half, step_delta, chol_vectors, copy_counts, parents)
+
+
 def solution(mesh):
     placed = (
         P(("rep", "chol"), "pop", None),
@@ -55,7 +397,7 @@
         P("rep"),
     )
     return jax.shard_map(
-        shards,
+        any_shards,
         mesh=mesh,
         in_specs=placed,
         out_specs=(P(("rep", "chol"), "pop", None), P(("rep", "pop"))),

time: 200 us -> 61.6 us (0.31)
  waiting for transfers between devices: 139 us -> 0 us
  Pallas kernels: 0 us -> 55.2 us
  blocking collectives: 22.4 us -> 0 us
  between operations: 13.8 us -> 0.65 us
  matrix products: 12.6 us -> 0 us
  other arithmetic: 6.49 us -> 0.63 us
    reduce_scatter x1 -> x0, waiting for transfers between devices: 86.7 us -> none  [child_forces(): lax.psum_scatter(factor * jnp.einsum('wgik,gil->kwl', cross_low, chol_vec...]
    pallas_call x0 -> x1, Pallas kernels: none -> 55.2 us  [ring_shards(): pl.pallas_call(functools.partial(step_kernel, n), out_shape=(jax.ShapeDty...]
    all_gather x1 -> x0, waiting for transfers between devices: 52 us -> none  [child_forces(): lax.all_gather(child_rows, 'chol', axis=0, tiled=True)]
    psum x1 -> x0, blocking collectives: 20.2 us -> none  [child_forces(): energies = lax.psum(trace_part, 'chol') * (-0.125 / (total_chol * orbitals))]
    dot_general x3 -> x0, matrix products: 12.6 us -> none  [the longest x1 5.82 us: child_forces(): jnp.einsum('wgik,gil->kwl', cross_low, chol_vectors, preferred_element_ty...]
    convert_element_type x3 -> x0, other arithmetic: 2.72 us -> none  [the longest x1 1.85 us: shards(): (picked.astype(jnp.float32) + step_delta.astype(jnp.float32)).astype(jnp....]
    dot_general x1 -> x0, local copies, waits for them, and re-layouts: 2.3 us -> none  [child_forces(): jnp.einsum('iwm,gkm->wgik', lax.all_gather(child_rows, 'chol', axis=0, ti...]
    reduce_sum x1, other arithmetic: 2.39 us -> 0.11 us  [ring_shards(): energy = jnp.sum(traces, axis=1) * (-0.125 / (n * vectors * orbitals))]
  transfers between devices with their start and end apart: 3 -> 0, of which waited for: 2 -> 0; matrix products, arithmetic and copies ran while one was open for 1% -> 0% of each run, Pallas kernels for 0% -> 0%
where the time goes in v1:
time: 61.6 us; the launch traced here: 61.4 us
  Pallas kernels  55.2 us (90%)
  local copies, waits for them, and re-layouts  4.89 us (8%)
  between operations  0.65 us (1%)
  other arithmetic  0.63 us (1%)
    pallas_call x1, Pallas kernels, ring_shards(): pl.pallas_call(functools.partial(step_kernel, n), out_shape=(jax.ShapeDty...  55.2 us
    unnamed x7, local copies, waits for them, and re-layouts  3.56 us
    transpose x1, local copies, waits for them, and re-layouts, ring_shards(): jnp.swapaxes(step_delta, 0, 1)  1.32 us

profile of v1, /device:TPU:0, one launch (start us, length us, event | category | flops | bytes accessed | tf_op | source)
XLA Modules:
  0.0 61.4 jit_solution(393284040241708030)
XLA Ops:
  0.6 1.3 %copy_bitcast_fusion = (bf16[8,16,1024]{2,1,0:T(8,128)(2,1)S(1)}, bf16[8,16,1024]{2,1,0:T(8,128)(2,1)S(1)}) fusion(bf16[16,8,1024]{2,1,0:T(8,128)(2,1)} %param.6, bf16[16,8,1024]{2,1,0:T(8,128)(2,1)} %param.5), kind=kLoop, calls=%fused_computation | loop fusion | bytes 1048576 | tf_op jit(solution)/shard_map/transpose | solution.py:367
  2.0 0.0 copy-start
  2.0 1.4 %copy-done = bf16[6,128,1024]{2,1,0:T(8,128)(2,1)S(1)} copy-done((bf16[6,128,1024]{2,1,0:T(8,128)(2,1)S(1)}, bf16[6,128,1024]{2,1,0:T(8,128)(2,1)}, u32[]{:S(2)}) %copy-start) | copy-done | bytes 1572888
  3.4 0.0 copy-start.1
  3.4 0.7 %copy-done.1 = s32[16]{0:T(128)S(1)} copy-done((s32[16]{0:T(128)S(1)}, s32[16]{0:T(128)}, u32[]{:S(2)}) %copy-start.1) | copy-done | bytes 88
  4.0 0.0 copy-start.2
  4.0 0.7 %copy-done.2 = s32[8]{0:T(128)S(1)} copy-done((s32[8]{0:T(128)S(1)}, s32[8]{0:T(128)}, u32[]{:S(2)}) %copy-start.2) | copy-done | bytes 56
  4.7 55.2 %shard_map.68 = (bf16[8,16,1024]{2,1,0:T(8,128)(2,1)S(1)}, f32[8,128]{1,0:T(8,128)S(1)}) custom-call(s32[16]{0:T(128)S(1)} %copy-done.1, s32[8]{0:T(128)S(1)} %copy-done.2, bf16[8,16,1024]{2,1,0:T(8,128)(2,1)S(1)} %get-tuple-element.9.green, bf16[8,16,1024]{2,1,0:T(8,128)(2,1)S(1)} %get-tuple-element.8.delta, bf16[6,128,1024]{2,1,0:T(8,128)(2,1)S(1)} %copy-done), custom_call_target="tpu_custom_call" | custom-call | flops 3221225472 | bytes 4194304 | tf_op jit(solution)/shard_map/pallas_call | solution.py:328
  59.9 0.9 %copy.9 = bf16[16,8,1024]{2,1,0:T(8,128)(2,1)} copy(bf16[16,8,1024]{2,0,1:T(8,128)(2,1)S(1)} %bitcast.5) | data formatting | bytes 524288
  60.8 0.1 reduce_sum.9
  60.9 0.5 broadcast_multiply_fusion
Async XLA Ops:
  2.0 1.4 %copy-start = (bf16[6,128,1024]{2,1,0:T(8,128)(2,1)S(1)}, bf16[6,128,1024]{2,1,0:T(8,128)(2,1)}, u32[]{:S(2)}) copy-start(bf16[6,128,1024]{2,1,0:T(8,128)(2,1)} %chol.1) | copy-start | bytes 4718596
  3.4 0.7 %copy-start.1 = (s32[16]{0:T(128)S(1)}, s32[16]{0:T(128)}, u32[]{:S(2)}) copy-start(s32[16]{0:T(128)} %parents.1) | copy-start | bytes 196
  4.0 0.7 %copy-start.2 = (s32[8]{0:T(128)S(1)}, s32[8]{0:T(128)}, u32[]{:S(2)}) copy-start(s32[8]{0:T(128)} %counts.1) | copy-start | bytes 100

commit v2 on v1

--- a/solution.py
+++ b/solution.py
@@ -62,11 +62,11 @@
 
 
 def step_kernel(
-    n, parents, counts, green, delta, chol, out, energy_out,
-    gpad, gall, cross, force, fsend, arrived, final, edge, traces,
-    ag_send, ag_recv, rs_send, rs_recv, tr_send, tr_recv, edge_send, edge_recv,
+    n, parents, counts, green_in, delta_in, chol_in, out, energy_out,
+    green, delta, chol, gpad, dturn, gall, cross, force, fsend, arrived, final, edge, traces,
+    ag_send, ag_recv, rs_send, rs_recv, tr_send, tr_recv, edge_send, edge_recv, load_sem,
 ):
-    walkers, rows, basis = green.shape
+    rows, walkers, basis = green.shape
     vectors, orbitals, _ = chol.shape
     chunks = walkers // CHUNK
     me = lax.axis_index("chol")
@@ -146,6 +146,13 @@
             device_id_type=MESH,
         )
 
+    loads = [
+        pltpu.make_async_copy(green_in, green, load_sem.at[0]),
+        pltpu.make_async_copy(delta_in, delta, load_sem.at[1]),
+        pltpu.make_async_copy(chol_in, chol, load_sem.at[2]),
+    ]
+    for load in loads:
+        load.start()
     barrier = pltpu.get_barrier_semaphore()
     for offset in range(1, n):
         pl.semaphore_signal(
@@ -153,11 +160,14 @@
         )
     pl.semaphore_signal(barrier, inc=1, device_id={"pop": 1 - pop}, device_id_type=MESH)
     gpad[pop * (walkers + 1)] = jnp.zeros((rows, basis), jnp.bfloat16)
-    gpad[pl.ds(1, walkers)] = green[...]
+    loads[0].wait()
+    gpad[pl.ds(1, walkers)] = jnp.swapaxes(green[...].astype(jnp.float32), 0, 1).astype(jnp.bfloat16)
+    loads[1].wait()
+    dturn[...] = jnp.swapaxes(delta[...].astype(jnp.float32), 0, 1)
     pl.semaphore_wait(barrier, n)
 
     edge_green = pltpu.make_async_remote_copy(
-        src_ref=green.at[(1 - pop) * (walkers - 1)],
+        src_ref=gpad.at[1 + (1 - pop) * (walkers - 1)],
         dst_ref=gpad.at[pop * (walkers + 1)],
         send_sem=edge_send.at[0],
         recv_sem=edge_recv.at[0],
@@ -165,7 +175,7 @@
         device_id_type=MESH,
     )
     edge_green_arrival = pltpu.make_async_remote_copy(
-        src_ref=green.at[(1 - pop) * (walkers - 1)],
+        src_ref=gpad.at[1 + (1 - pop) * (walkers - 1)],
         dst_ref=gpad.at[(1 - pop) * (walkers + 1)],
         send_sem=edge_send.at[0],
         recv_sem=edge_recv.at[0],
@@ -181,7 +191,7 @@
         for j in range(CHUNK):
             child = pop * walkers + w0 + j
             parent = parents[child]
-            row = delta[w0 + j].astype(jnp.float32)
+            row = dturn[w0 + j]
             for k in range(3):
                 chosen = jnp.where(parent == child - 1 + k, 1.0, 0.0)
                 row = row + chosen * gpad[w0 + j + k].astype(jnp.float32)
@@ -200,10 +210,17 @@
 
         lax.fori_loop(0, chunks, forward, 0)
 
+    loads[2].wait()
     row_ids = lax.broadcasted_iota(jnp.int32, (orbitals, 2 * orbitals), 0)
     col_ids = lax.broadcasted_iota(jnp.int32, (orbitals, 2 * orbitals), 1)
     diagonal = (row_ids == col_ids) | (row_ids + orbitals == col_ids)
     walker_ids = lax.broadcasted_iota(jnp.int32, (walkers, orbitals), 0)
+
+    def add_and_forward(ch, step):
+        for chain in range(2):
+            if step < hops[chain]:
+                scatter(ch, chain, step - 1).wait_recv()
+                start_scatter(ch, chain, step)
 
     def compute(ch, total):
         for chain in range(2):
@@ -239,22 +256,25 @@
         ).reshape(CHUNK, orbitals, basis)
         for chain in range(2):
             start_scatter(ch, chain, 0)
+
+        @pl.when(ch > 0)
+        def _():
+            add_and_forward(ch - 1, 1)
+
         return total
 
     traces[me] = lax.fori_loop(0, chunks, compute, jnp.zeros((walkers, orbitals), jnp.float32))
     for offset in range(1, n):
         trace_copy(offset - 1, me, lax.rem(me + offset, n)).start()
 
-    for step in range(1, hops[0]):
-
-        def add_and_forward(ch, carry, step=step):
-            for chain in range(2):
-                if step < hops[chain]:
-                    scatter(ch, chain, step - 1).wait_recv()
-                    start_scatter(ch, chain, step)
+    add_and_forward(jnp.int32(chunks - 1), 1)
+    for step in range(2, hops[0]):
+
+        def one_chunk(ch, carry, step=step):
+            add_and_forward(ch, step)
             return carry
 
-        lax.fori_loop(0, chunks, add_and_forward, 0)
+        lax.fori_loop(0, chunks, one_chunk, 0)
 
     edge_force = pltpu.make_async_remote_copy(
         src_ref=edge.at[0],
@@ -319,6 +339,7 @@
     n = lax.axis_size("chol")
     rows, walkers, basis = green_half.shape
     vectors, orbitals, _ = chol_vectors.shape
+    hbm = pl.BlockSpec(memory_space=pltpu.HBM)
     chunks = walkers // CHUNK
     hops = n // 2
     smem = pl.BlockSpec(memory_space=pltpu.SMEM)
@@ -331,10 +352,14 @@
             jax.ShapeDtypeStruct((walkers, rows, basis), jnp.bfloat16),
             jax.ShapeDtypeStruct((walkers, orbitals), jnp.float32),
         ),
-        in_specs=[smem, smem, vmem, vmem, vmem],
+        in_specs=[smem, smem, hbm, hbm, hbm],
         out_specs=(vmem, vmem),
         scratch_shapes=[
+            pltpu.VMEM(green_half.shape, jnp.bfloat16),
+            pltpu.VMEM(green_half.shape, jnp.bfloat16),
+            pltpu.VMEM(chol_vectors.shape, jnp.bfloat16),
             pltpu.VMEM((walkers + 2, rows, basis), jnp.bfloat16),
+            pltpu.VMEM((walkers, rows, basis), jnp.float32),
             pltpu.VMEM((walkers, orbitals, basis), jnp.bfloat16),
             pltpu.VMEM((CHUNK * orbitals, wide), jnp.bfloat16),
             pltpu.VMEM((walkers, orbitals, basis), jnp.float32),
@@ -351,9 +376,10 @@
             dma((n - 1,)),
             dma((2,)),
             dma((2,)),
+            dma((3,)),
         ],
         compiler_params=pltpu.CompilerParams(
-            collective_id=0, has_side_effects=True, vmem_limit_bytes=40 * 1024 * 1024
+            collective_id=0, has_side_effects=True, vmem_limit_bytes=63 * 1024 * 1024
         ),
         cost_estimate=pl.CostEstimate(
             flops=4 * walkers * orbitals * wide * basis,
@@ -363,8 +389,8 @@
     )(
         parents,
         copy_counts,
-        jnp.swapaxes(green_half, 0, 1),
-        jnp.swapaxes(step_delta, 0, 1),
+        green_half,
+        step_delta,
         chol_vectors,
     )
     energy = jnp.sum(traces, axis=1) * (-0.125 / (n * vectors * orbitals))

time: 61.6 us -> 59.8 us (0.971)
  local copies, waits for them, and re-layouts: 4.89 us -> 1.8 us
  Pallas kernels: 55.2 us -> 55.9 us
  other arithmetic: 0.63 us -> 1.3 us
    unnamed x7 -> x1, local copies, waits for them, and re-layouts: 3.56 us -> 1.8 us
    transpose x1 -> x0, local copies, waits for them, and re-layouts: 1.32 us -> none  [ring_shards(): jnp.swapaxes(step_delta, 0, 1)]
    reduce_sum x1, other arithmetic: 0.11 us -> 0.79 us  [ring_shards(): energy = jnp.sum(traces, axis=1) * (-0.125 / (n * vectors * orbitals))]
    pallas_call x1, Pallas kernels: 55.2 us -> 55.9 us  [ring_shards(): pl.pallas_call(functools.partial(step_kernel, n), out_shape=(jax.ShapeDty...]
where the time goes in v2:
time: 59.8 us; the launch traced here: 59.6 us
  Pallas kernels  55.9 us (93%)
  local copies, waits for them, and re-layouts  1.8 us (3%)
  other arithmetic  1.3 us (2%)
  between operations  0.64 us (1%)
    pallas_call x1, Pallas kernels, ring_shards(): pl.pallas_call(functools.partial(step_kernel, n), out_shape=(jax.ShapeDty...  55.9 us
    unnamed x1, local copies, waits for them, and re-layouts  1.8 us

profile of v2, /device:TPU:0, one launch (start us, length us, event | category | flops | bytes accessed | tf_op | source)
XLA Modules:
  0.0 59.6 jit_solution(437751382976315487)
XLA Ops:
  0.6 55.9 %shard_map.68 = (bf16[8,16,1024]{2,1,0:T(8,128)(2,1)}, f32[8,128]{1,0:T(8,128)}) custom-call(s32[16]{0:T(128)} %parents.1, s32[8]{0:T(128)} %counts.1, bf16[16,8,1024]{2,1,0:T(8,128)(2,1)} %green_in.1, bf16[16,8,1024]{2,1,0:T(8,128)(2,1)} %delta_in.1, bf16[6,128,1024]{2,1,0:T(8,128)(2,1)} %chol_in.1), custom_call_target="tpu_custom_call" | custom-call | flops 3221225472 | bytes 4194304 | tf_op jit(solution)/shard_map/pallas_call | solution.py:349
  56.5 1.8 %copy.7 = bf16[16,8,1024]{2,1,0:T(8,128)(2,1)} copy(bf16[16,8,1024]{2,0,1:T(8,128)(2,1)} %bitcast.1) | data formatting | bytes 524288
  58.3 0.8 %reduce_sum.9 = f32[8]{0:T(128)S(1)} reduce(f32[8,128]{1,0:T(8,128)} %get-tuple-element.5, f32[]{:T(128)} %constant.0.clone.1), dimensions={1}, to_apply=%region_0.0 | reduce | flops 1016 | bytes 4132 | tf_op jit(solution)/shard_map/reduce_sum | solution.py:396
  59.1 0.5 broadcast_multiply_fusion

commit v3 on v2

--- a/solution.py
+++ b/solution.py
@@ -184,10 +184,8 @@
     )
     edge_green.start()
 
-    for ch in range(chunks):
-        if ch == 1:
-            edge_green_arrival.wait_recv()
-        w0 = first_walker(jnp.int32(ch))
+    def make_children(ch):
+        w0 = first_walker(ch)
         for j in range(CHUNK):
             child = pop * walkers + w0 + j
             parent = parents[child]
@@ -197,18 +195,13 @@
                 row = row + chosen * gpad[w0 + j + k].astype(jnp.float32)
             gall[w0 + j, orbital_rows(me), :] = row.astype(jnp.bfloat16)
         for chain in range(2):
-            gather(jnp.int32(ch), chain, 0).start()
-
-    for step in range(1, hops[0]):
-
-        def forward(ch, carry, step=step):
-            for chain in range(2):
-                if step < hops[chain]:
-                    gather_arrival(ch, chain, step - 1).wait_recv()
-                    gather(ch, chain, step).start()
-            return carry
-
-        lax.fori_loop(0, chunks, forward, 0)
+            gather(ch, chain, 0).start()
+
+    def forward(ch, step):
+        for chain in range(2):
+            if step < hops[chain]:
+                gather_arrival(ch, chain, step - 1).wait_recv()
+                gather(ch, chain, step).start()
 
     loads[2].wait()
     row_ids = lax.broadcasted_iota(jnp.int32, (orbitals, 2 * orbitals), 0)
@@ -222,7 +215,7 @@
                 scatter(ch, chain, step - 1).wait_recv()
                 start_scatter(ch, chain, step)
 
-    def compute(ch, total):
+    def compute(ch):
         for chain in range(2):
             gather_arrival(ch, chain, hops[chain] - 1).wait_recv()
         w0 = first_walker(ch)
@@ -248,7 +241,7 @@
             )
             line = jnp.sum(jnp.where(diagonal, products, 0.0), axis=0, keepdims=True)
             line = line[:, :orbitals] + line[:, orbitals:]
-            total = total + jnp.where(walker_ids == w0 + j, line, 0.0)
+            traces[me] = traces[me] + jnp.where(walker_ids == w0 + j, line, 0.0)
         force[pl.ds(w0, CHUNK)] = jnp.dot(
             cross[...],
             chol[...].reshape(vectors * orbitals, basis),
@@ -257,24 +250,60 @@
         for chain in range(2):
             start_scatter(ch, chain, 0)
 
-        @pl.when(ch > 0)
-        def _():
-            add_and_forward(ch - 1, 1)
-
-        return total
-
-    traces[me] = lax.fori_loop(0, chunks, compute, jnp.zeros((walkers, orbitals), jnp.float32))
+    traces[me] = jnp.zeros((walkers, orbitals), jnp.float32)
+    last = hops[0]
+    delay = last - 1
+    half = chunks // 2
+    order = [last] + list(range(last)) + list(range(last + 1, 2 * last))
+
+    def tick(now, carry):
+        for stage in order:
+
+            @pl.when((now == stage) | (now == stage + delay))
+            def _(stage=stage):
+                base = half * lax.div(now - stage, delay)
+
+                def one_chunk(c, inner):
+                    ch = base + c
+                    if stage == 0:
+
+                        @pl.when(ch == 1)
+                        def _():
+                            edge_green_arrival.wait_recv()
+
+                        make_children(ch)
+                    elif stage < last:
+                        forward(ch, stage)
+                    elif stage == last:
+                        compute(ch)
+                    else:
+                        add_and_forward(ch, stage - last)
+                    return inner
+
+                lax.fori_loop(0, half, one_chunk, 0)
+
+        return carry
+
+    lax.fori_loop(0, last + delay + 1, tick, 0)
     for offset in range(1, n):
         trace_copy(offset - 1, me, lax.rem(me + offset, n)).start()
 
-    add_and_forward(jnp.int32(chunks - 1), 1)
-    for step in range(2, hops[0]):
-
-        def one_chunk(ch, carry, step=step):
-            add_and_forward(ch, step)
-            return carry
-
-        lax.fori_loop(0, chunks, one_chunk, 0)
+    def late_tick(now, carry):
+        for stage in range(last + 1, 2 * last):
+
+            @pl.when((now == stage) | (now == stage + delay))
+            def _(stage=stage):
+                base = half * lax.div(now - stage, delay)
+
+                def one_chunk(c, inner):
+                    add_and_forward(base + c, stage - last)
+                    return inner
+
+                lax.fori_loop(0, half, one_chunk, 0)
+
+        return carry
+
+    lax.fori_loop(last + delay + 1, 2 * last + delay, late_tick, 0)
 
     edge_force = pltpu.make_async_remote_copy(
         src_ref=edge.at[0],
@@ -285,9 +314,47 @@
         device_id_type=MESH,
     )
     final[pop * (walkers + 1)] = jnp.zeros((rows, basis), jnp.float32)
+
+    def parent_row(order_index):
+        w = pop * order_index + (1 - pop) * (walkers - 1 - order_index)
+        parent = pop * walkers + w
+        row = jnp.zeros((rows, basis), jnp.float32)
+        for k in range(3):
+            child = parent - 1 + k
+            inside = (child >= 0) & (child < 2 * walkers)
+            taken = parents[jnp.minimum(jnp.maximum(child, 0), 2 * walkers - 1)] == parent
+            row = row + jnp.where(inside & taken, 1.0, 0.0) * final[w + k]
+        copies = jnp.maximum(counts[w], 1).astype(jnp.float32)
+        out[w] = (row / jnp.full((rows, basis), copies)).astype(jnp.bfloat16)
+
+    early = walkers - CHUNK - 1
     for ch in range(chunks):
         at = jnp.int32(ch)
         w0 = first_walker(at)
+        if ch == chunks - 1:
+            edge_force.wait_recv()
+            final[(1 - pop) * (walkers + 1)] = edge[1].astype(jnp.float32)
+            for i in range(early):
+                parent_row(i)
+            for offset in range(1, n):
+                trace_copy(offset - 1, lax.rem(me + n - offset, n), me).wait_recv()
+            energy = traces[0]
+            for i in range(1, n):
+                energy = energy + traces[i]
+            energy = jnp.sum(energy, axis=1, keepdims=True) * (-0.125 / (n * vectors * orbitals))
+            energy_out[...] = jnp.broadcast_to(energy, energy_out.shape)
+            edge_green.wait_send()
+            edge_force.wait_send()
+            for offset in range(1, n):
+                trace_copy(offset - 1, me, lax.rem(me + offset, n)).wait_send()
+
+            def drain(c, carry):
+                for chain in range(2):
+                    for step in range(hops[chain]):
+                        gather(c, chain, step).wait_send()
+                return carry
+
+            lax.fori_loop(0, chunks, drain, 0)
         for chain in range(2):
             scatter(at, chain, hops[chain] - 1).wait_recv()
         for j in range(CHUNK):
@@ -300,39 +367,16 @@
             edge[0] = final[1 + (1 - pop) * (walkers - 1)].astype(jnp.bfloat16)
             edge_force.start()
 
-    edge_force.wait_recv()
-    final[(1 - pop) * (walkers + 1)] = edge[1].astype(jnp.float32)
-    for w in range(walkers):
-        parent = pop * walkers + w
-        row = jnp.zeros((rows, basis), jnp.float32)
-        for k in range(3):
-            child = parent - 1 + k
-            inside = (child >= 0) & (child < 2 * walkers)
-            taken = parents[jnp.minimum(jnp.maximum(child, 0), 2 * walkers - 1)] == parent
-            row = row + jnp.where(inside & taken, 1.0, 0.0) * final[w + k]
-        copies = jnp.maximum(counts[w], 1).astype(jnp.float32)
-        out[w] = (row / jnp.full((rows, basis), copies)).astype(jnp.bfloat16)
-
-    for offset in range(1, n):
-        trace_copy(offset - 1, lax.rem(me + n - offset, n), me).wait_recv()
-    energy = traces[0]
-    for i in range(1, n):
-        energy = energy + traces[i]
-    energy_out[...] = energy
-
-    edge_green.wait_send()
-    edge_force.wait_send()
-    for offset in range(1, n):
-        trace_copy(offset - 1, me, lax.rem(me + offset, n)).wait_send()
-
-    def drain(ch, carry):
+    for i in range(early, walkers):
+        parent_row(i)
+
+    def drain_sums(c, carry):
         for chain in range(2):
             for step in range(hops[chain]):
-                gather(ch, chain, step).wait_send()
-                scatter(ch, chain, step).wait_send()
+                scatter(c, chain, step).wait_send()
         return carry
 
-    lax.fori_loop(0, chunks, drain, 0)
+    lax.fori_loop(0, chunks, drain_sums, 0)
 
 
 def ring_shards(green_half, step_delta, chol_vectors, copy_counts, parents):
@@ -379,7 +423,7 @@
             dma((3,)),
         ],
         compiler_params=pltpu.CompilerParams(
-            collective_id=0, has_side_effects=True, vmem_limit_bytes=63 * 1024 * 1024
+            collective_id=0, has_side_effects=True, vmem_limit_bytes=62 * 1024 * 1024
         ),
         cost_estimate=pl.CostEstimate(
             flops=4 * walkers * orbitals * wide * basis,
@@ -393,8 +437,7 @@
         step_delta,
         chol_vectors,
     )
-    energy = jnp.sum(traces, axis=1) * (-0.125 / (n * vectors * orbitals))
-    return jnp.swapaxes(out, 0, 1), energy
+    return jnp.swapaxes(out, 0, 1), traces[:, 0]
 
 
 def any_shards(green_half, step_delta, chol_vectors, copy_counts, parents):

time: 59.8 us -> 64 us (1.070)
  Pallas kernels: 55.9 us -> 60.1 us
  other arithmetic: 1.3 us -> 0 us
  local copies, waits for them, and re-layouts: 1.8 us -> 3.1 us
    pallas_call x1, Pallas kernels: 55.9 us -> 60.1 us  [ring_shards(): pl.pallas_call(functools.partial(step_kernel, n), out_shape=(jax.ShapeDty...]
    slice x0 -> x1, local copies, waits for them, and re-layouts: none -> 1.3 us  [ring_shards(): return (jnp.swapaxes(out, 0, 1), traces[:, 0])]
    reduce_sum x1 -> x0, other arithmetic: 0.79 us -> none  [ring_shards(): energy = jnp.sum(traces, axis=1) * (-0.125 / (n * vectors * orbitals))]
where the time goes in v3:
time: 64 us; the launch traced here: 63.8 us
  Pallas kernels  60.1 us (94%)
  local copies, waits for them, and re-layouts  3.1 us (5%)
  between operations  0.64 us (1%)
    pallas_call x1, Pallas kernels, ring_shards(): pl.pallas_call(functools.partial(step_kernel, n), out_shape=(jax.ShapeDty...  60.1 us
    unnamed x1, local copies, waits for them, and re-layouts  1.8 us
    slice x1, local copies, waits for them, and re-layouts, ring_shards(): return (jnp.swapaxes(out, 0, 1), traces[:, 0])  1.3 us

profile of v3, /device:TPU:0, one launch (start us, length us, event | category | flops | bytes accessed | tf_op | source)
XLA Modules:
  0.0 63.8 jit_solution(8845809186599470649)
XLA Ops:
  0.6 60.1 %shard_map.68 = (bf16[8,16,1024]{2,1,0:T(8,128)(2,1)}, f32[8,128]{1,0:T(8,128)}) custom-call(s32[16]{0:T(128)} %parents.1, s32[8]{0:T(128)} %counts.1, bf16[16,8,1024]{2,1,0:T(8,128)(2,1)} %green_in.1, bf16[16,8,1024]{2,1,0:T(8,128)(2,1)} %delta_in.1, bf16[6,128,1024]{2,1,0:T(8,128)(2,1)} %chol_in.1), custom_call_target="tpu_custom_call" | custom-call | flops 3221225472 | bytes 4194304 | tf_op jit(solution)/shard_map/pallas_call | solution.py:393
  60.7 1.8 %copy.8 = bf16[16,8,1024]{2,1,0:T(8,128)(2,1)} copy(bf16[16,8,1024]{2,0,1:T(8,128)(2,1)} %bitcast.1) | data formatting | bytes 524288
  62.5 1.3 %slice_reduce_fusion = f32[8]{0:T(128)} fusion(f32[8,128]{1,0:T(8,128)} %get-tuple-element.5), kind=kLoop, calls=%fused_computation | loop fusion | bytes 64 | tf_op jit(solution)/shard_map/slice | solution.py:440

commit v4 on v3

--- a/solution.py
+++ b/solution.py
@@ -252,58 +252,37 @@
 
     traces[me] = jnp.zeros((walkers, orbitals), jnp.float32)
     last = hops[0]
-    delay = last - 1
-    half = chunks // 2
-    order = [last] + list(range(last)) + list(range(last + 1, 2 * last))
-
-    def tick(now, carry):
-        for stage in order:
-
-            @pl.when((now == stage) | (now == stage + delay))
-            def _(stage=stage):
-                base = half * lax.div(now - stage, delay)
-
-                def one_chunk(c, inner):
-                    ch = base + c
-                    if stage == 0:
-
-                        @pl.when(ch == 1)
-                        def _():
-                            edge_green_arrival.wait_recv()
-
-                        make_children(ch)
-                    elif stage < last:
-                        forward(ch, stage)
-                    elif stage == last:
-                        compute(ch)
-                    else:
-                        add_and_forward(ch, stage - last)
-                    return inner
-
-                lax.fori_loop(0, half, one_chunk, 0)
-
-        return carry
-
-    lax.fori_loop(0, last + delay + 1, tick, 0)
+
+    def per_chunk(act):
+        def body(ch, carry):
+            act(ch)
+            return carry
+
+        lax.fori_loop(0, chunks, body, 0)
+
+    def begin(ch):
+        @pl.when(ch == 1)
+        def _():
+            edge_green_arrival.wait_recv()
+
+        make_children(ch)
+
+    def compute_and_sum(ch):
+        compute(ch)
+
+        @pl.when(ch > 0)
+        def _():
+            add_and_forward(ch - 1, 1)
+
+    per_chunk(begin)
+    for step in range(1, last):
+        per_chunk(functools.partial(forward, step=step))
+    per_chunk(compute_and_sum)
     for offset in range(1, n):
         trace_copy(offset - 1, me, lax.rem(me + offset, n)).start()
-
-    def late_tick(now, carry):
-        for stage in range(last + 1, 2 * last):
-
-            @pl.when((now == stage) | (now == stage + delay))
-            def _(stage=stage):
-                base = half * lax.div(now - stage, delay)
-
-                def one_chunk(c, inner):
-                    add_and_forward(base + c, stage - last)
-                    return inner
-
-                lax.fori_loop(0, half, one_chunk, 0)
-
-        return carry
-
-    lax.fori_loop(last + delay + 1, 2 * last + delay, late_tick, 0)
+    add_and_forward(jnp.int32(chunks - 1), 1)
+    for step in range(2, last):
+        per_chunk(functools.partial(add_and_forward, step=step))
 
     edge_force = pltpu.make_async_remote_copy(
         src_ref=edge.at[0],
@@ -423,7 +402,7 @@
             dma((3,)),
         ],
         compiler_params=pltpu.CompilerParams(
-            collective_id=0, has_side_effects=True, vmem_limit_bytes=62 * 1024 * 1024
+            collective_id=0, has_side_effects=True, vmem_limit_bytes=63 * 1024 * 1024
         ),
         cost_estimate=pl.CostEstimate(
             flops=4 * walkers * orbitals * wide * basis,

time: 64 us -> 59.7 us (0.933)
  Pallas kernels: 60.1 us -> 55.8 us
    pallas_call x1, Pallas kernels: 60.1 us -> 55.8 us  [ring_shards(): pl.pallas_call(functools.partial(step_kernel, n), out_shape=(jax.ShapeDty...]
where the time goes in v4:
time: 59.7 us; the launch traced here: 59.5 us
  Pallas kernels  55.8 us (93%)
  local copies, waits for them, and re-layouts  3.1 us (5%)
  between operations  0.64 us (1%)
    pallas_call x1, Pallas kernels, ring_shards(): pl.pallas_call(functools.partial(step_kernel, n), out_shape=(jax.ShapeDty...  55.8 us
    unnamed x1, local copies, waits for them, and re-layouts  1.8 us
    slice x1, local copies, waits for them, and re-layouts, ring_shards(): return (jnp.swapaxes(out, 0, 1), traces[:, 0])  1.3 us

profile of v4, /device:TPU:0, one launch (start us, length us, event | category | flops | bytes accessed | tf_op | source)
XLA Modules:
  0.0 59.5 jit_solution(11287947539151277456)
XLA Ops:
  0.6 55.8 %shard_map.68 = (bf16[8,16,1024]{2,1,0:T(8,128)(2,1)}, f32[8,128]{1,0:T(8,128)}) custom-call(s32[16]{0:T(128)} %parents.1, s32[8]{0:T(128)} %counts.1, bf16[16,8,1024]{2,1,0:T(8,128)(2,1)} %green_in.1, bf16[16,8,1024]{2,1,0:T(8,128)(2,1)} %delta_in.1, bf16[6,128,1024]{2,1,0:T(8,128)(2,1)} %chol_in.1), custom_call_target="tpu_custom_call" | custom-call | flops 3221225472 | bytes 4194304 | tf_op jit(solution)/shard_map/pallas_call | solution.py:372
  56.4 1.8 %copy.8 = bf16[16,8,1024]{2,1,0:T(8,128)(2,1)} copy(bf16[16,8,1024]{2,0,1:T(8,128)(2,1)} %bitcast.1) | data formatting | bytes 524288
  58.2 1.3 %slice_reduce_fusion = f32[8]{0:T(128)} fusion(f32[8,128]{1,0:T(8,128)} %get-tuple-element.5), kind=kLoop, calls=%fused_computation | loop fusion | bytes 64 | tf_op jit(solution)/shard_map/slice | solution.py:419
